TPU v7x, 256 devices: a whole 4x4x8 slice. The times are simulated.
256 devices in a mesh: ctx: 32 (over x, z), head: 8 (over y, core).
Axes of the slice: x: 4, y: 4, z: 8, core: 2. Of those that a mesh axis runs over, the one named last changes fastest.
Arguments:
- queries: bfloat16 [16384, 4096], P('ctx', 'head'), may hold values from -5 to 5
- key_rows: bfloat16 [16384, 1024], P('ctx', 'head'), may hold values from -5 to 5
- value_rows: bfloat16 [16384, 1024], P('ctx', 'head'), may hold values from -6 to 6
- slash_offsets: int32 [32, 4], P('head'), may hold values from 0 to 8, as said below
- union_blocks: int32 [8, 32, 2], P('head'), may hold values from 0 to 7, as said below
- head_picks: int32 [32, 32, 1], P('head'), may hold values from 0 to 1, as said below
- owner_counts: int32 [32, 32], P('head'), may hold values from 0 to 1, as said below
- out_weight: bfloat16 [4096, 4096], P(None, 'head'), may hold values from -0.09375 to 0.09375
Outputs:
- projected: bfloat16 [16384, 4096], P('ctx', 'head')
Inputs may be any that keep to these rules, and one draw needn't show every extreme that they name: `slash_offsets`: each head's offsets are distinct and include 0 and 8. `union_blocks`: the 2 entries of each KV head and sequence block are distinct. `head_picks`: the 1 entries of each query head and sequence block are distinct. `owner_counts`: equal to 1 for sequence block 0.
All inputs are finite; a program needn't handle non-finite values.
Results may differ from a plain program's by a relative error of at most 0.0056.
Values may be sent and summed in bfloat16 or wider, within the bound.
A program may use at most 128 MiB of HBM per device.

v0:
```python
import jax
import jax.numpy as jnp
from jax import lax
from jax.sharding import PartitionSpec as P

HEAD_SIZE = 128
BLOCK_TOKENS = 64
NS = 4
VPER = 1


def from_behind(array, axis, by):
    length = lax.axis_size(axis)
    pairs = [(i, i + by) for i in range(length) if 0 <= i + by < length]
    return lax.ppermute(array, axis, pairs)


def attend(
    vert_scores, vert_mask, diagonal_scores, slash_mask, vert_values, diagonal_values, per_dev
):
    masked_vert = jnp.where(vert_mask, vert_scores, -1e30)
    masked_slash = jnp.where(slash_mask, diagonal_scores, -1e30)
    peak = jnp.maximum(
        jnp.max(masked_vert, axis=-1, keepdims=True), jnp.max(masked_slash, axis=-1, keepdims=True)
    )
    weight_vert = jnp.exp(masked_vert - peak)
    weight_slash = jnp.exp(masked_slash - peak)
    total = jnp.sum(weight_vert, axis=-1, keepdims=True) + jnp.sum(
        weight_slash, axis=-1, keepdims=True
    )
    prob_vert = weight_vert.astype(jnp.bfloat16)
    slash_probability = weight_slash.astype(jnp.bfloat16).reshape(
        per_dev, BLOCK_TOKENS, NS, BLOCK_TOKENS
    )
    numer = jnp.dot(prob_vert, vert_values, preferred_element_type=jnp.float32)
    diagonal_portion = jnp.einsum(
        "wojf,wjfl->wol", slash_probability, diagonal_values, preferred_element_type=jnp.float32
    )
    numer = numer + diagonal_portion.reshape(per_dev * BLOCK_TOKENS, HEAD_SIZE)
    return (numer / total).astype(jnp.bfloat16)


def shards(
    queries, key_rows, value_rows, slash_offsets, union_blocks, head_picks, owner_counts, out_weight
):
    tokens = queries.shape[0]
    per_dev = tokens // BLOCK_TOKENS
    heads_here = slash_offsets.shape[0]
    groups_here = key_rows.shape[1] // HEAD_SIZE
    group_size = heads_here // groups_here
    owners = lax.axis_size("ctx")
    device_rank = lax.axis_index("ctx")
    scale_of_scores = jnp.float32(HEAD_SIZE ** (-0.5))
    stacked = jnp.stack([key_rows, value_rows])
    previous = from_behind(stacked, "ctx", 1)
    extended = jnp.concatenate([previous, stacked], axis=1).reshape(
        2, 2 * per_dev, BLOCK_TOKENS, groups_here, HEAD_SIZE
    )
    local_blocks = stacked.reshape(2, per_dev, BLOCK_TOKENS, groups_here, HEAD_SIZE)
    head_group = jnp.arange(heads_here, dtype=jnp.int32) // group_size
    mine_union = lax.dynamic_index_in_dim(union_blocks, device_rank, 1, keepdims=False)
    owner_base = jnp.arange(owners, dtype=jnp.int32)[:, None] * per_dev
    slot_rank = jnp.arange(VPER, dtype=jnp.int32)
    chosen = slot_rank[None, None, :] < owner_counts[:, :, None]
    mine_picks = lax.dynamic_index_in_dim(head_picks, device_rank, 1, keepdims=False)
    chosen_local = jnp.take_along_axis(mine_union[head_group], mine_picks, axis=1)
    block_rows = local_blocks[:, chosen_local, :, head_group[:, None], :]
    gathered = lax.all_gather(block_rows[:, None], "ctx", axis=1, tiled=True)
    slot_block = owner_base[None] + jnp.take_along_axis(
        union_blocks[head_group], head_picks, axis=2
    )
    source_of = list(range(heads_here))
    query_place = device_rank * tokens + jnp.arange(tokens, dtype=jnp.int32)
    query_block = device_rank * per_dev + jnp.arange(per_dev, dtype=jnp.int32)
    inner_offset = jnp.arange(BLOCK_TOKENS, dtype=jnp.int32)
    local_index = jnp.arange(per_dev, dtype=jnp.int32)
    per_head = []
    for head_index in range(heads_here):
        kv_index = head_index // group_size
        offsets = slash_offsets[head_index]
        query_head = queries[:, head_index * HEAD_SIZE : (head_index + 1) * HEAD_SIZE]
        vertical = gathered[source_of[head_index]]
        blocks_flat = slot_block[head_index].reshape(-1)
        valid_flat = chosen[head_index].reshape(-1)
        slot_count = blocks_flat.shape[0]
        vert_keys = vertical[:, :, 0].reshape(slot_count * BLOCK_TOKENS, HEAD_SIZE)
        vert_values = vertical[:, :, 1].reshape(slot_count * BLOCK_TOKENS, HEAD_SIZE)
        vert_scores = (
            jnp.einsum("qd,kd->qk", query_head, vert_keys, preferred_element_type=jnp.float32)
            * scale_of_scores
        )
        distance = query_block[:, None] - blocks_flat[None, :]
        on_slash = jnp.any(distance[:, :, None] == offsets[None, None, :], axis=2)
        block_mask = valid_flat[None, :] & jnp.logical_not(on_slash)
        key_place = (blocks_flat[:, None] * BLOCK_TOKENS + inner_offset[None, :]).reshape(-1)
        vert_mask = jnp.broadcast_to(
            block_mask[:, None, :, None], (per_dev, BLOCK_TOKENS, slot_count, BLOCK_TOKENS)
        ).reshape(tokens, slot_count * BLOCK_TOKENS)
        vert_mask = vert_mask & (key_place[None, :] <= query_place[:, None])
        group_slab = extended[:, :, :, kv_index, :]
        ext_index = local_index[:, None] + per_dev - offsets[None, :]
        slash_rows = group_slab[:, ext_index]
        diagonal_scores = (
            jnp.einsum(
                "hax,hisx->hais",
                query_head.reshape(per_dev, BLOCK_TOKENS, HEAD_SIZE),
                slash_rows[0],
                preferred_element_type=jnp.float32,
            )
            * scale_of_scores
        )
        slash_valid = query_block[:, None] - offsets[None, :] >= 0
        slash_mask = slash_valid[:, None, :, None] & (
            (offsets[None, None, :, None] > 0)
            | (inner_offset[None, None, None, :] <= inner_offset[None, :, None, None])
        )
        slash_mask = slash_mask.reshape(tokens, NS * BLOCK_TOKENS)
        per_head.append(
            attend(
                vert_scores,
                vert_mask,
                diagonal_scores.reshape(tokens, NS * BLOCK_TOKENS),
                slash_mask,
                vert_values,
                slash_rows[1],
                per_dev,
            )
        )
    attended = jnp.concatenate(per_head, axis=1)
    projected = jnp.dot(
        lax.all_gather(attended, "head", axis=1, tiled=True),
        out_weight,
        preferred_element_type=jnp.float32,
    )
    return projected.astype(jnp.bfloat16)


def solution(mesh):
    in_specs = (
        P("ctx", "head"),
        P("ctx", "head"),
        P("ctx", "head"),
        P("head", None),
        P("head", None, None),
        P("head", None, None),
        P("head", None),
        P(None, "head"),
    )
    out_specs = P("ctx", "head")
    return jax.shard_map(shards, mesh=mesh, in_specs=in_specs, out_specs=out_specs, check_vma=False)
```

profile of v0, /device:TPU:1, one launch (start us, length us, event | category | flops | bytes accessed | tf_op | source)
XLA Modules:
  0.0 189.1 jit_solution(1846127941252690670)
XLA Ops:
  12.4 4.4 %collective-permute-start = (bf16[2,512,128]{2,1,0:T(8,128)(2,1)S(1)}, bf16[2,512,128]{2,1,0:T(8,128)(2,1)S(1)}, u32[]{:S(2)}, u32[]{:S(2)}) collective-permute-start(bf16[2,512,128]{2,1,0:T(8,128)(2,1)S(1)} %pad_maximum_fusion.2), channel_id=1, source_target_pairs={{0,8},{8,16},{16,24},{24,32},{32,40},{40,48},{48,56},{56,64},{64,7... | collective-permute-start | bytes 786440 | tf_op jit(solution)/shard_map/ppermute | solution.py:15
  18.3 1.5 gather_fusion.5
  23.7 4.7 %reshape.1051 = pred[512,2048]{0,1:T(32,128)(4,1)} reshape(pred[8,64,32,64]{1,0,3,2:T(8,128)(4,1)S(1)} %broadcast_in_dim.29) | data formatting | bytes 2097152 | tf_op jit(solution)/shard_map/reshape | solution.py:98
  29.8 4.7 %reshape.1054 = pred[512,2048]{0,1:T(32,128)(4,1)} reshape(pred[8,64,32,64]{1,0,3,2:T(8,128)(4,1)S(1)} %broadcast_in_dim.33) | data formatting | bytes 2097152 | tf_op jit(solution)/shard_map/reshape | solution.py:98
  35.9 4.7 %reshape.1057 = pred[512,2048]{0,1:T(32,128)(4,1)} reshape(pred[8,64,32,64]{1,0,3,2:T(8,128)(4,1)S(1)} %broadcast_in_dim.34) | data formatting | bytes 2097152 | tf_op jit(solution)/shard_map/reshape | solution.py:98
  42.0 4.7 %reshape.1060 = pred[512,2048]{0,1:T(32,128)(4,1)} reshape(pred[8,64,32,64]{1,0,3,2:T(8,128)(4,1)S(1)} %broadcast_in_dim.35) | data formatting | bytes 2097152 | tf_op jit(solution)/shard_map/reshape | solution.py:98
  50.0 1.3 fusion.107
  57.2 1.7 gather_fusion.4
  58.9 1.3 copy.70
  61.6 32.7 %all-gather.6.cloned.1.call-done = bf16[4,64,64,128]{3,2,1,0:T(8,128)(2,1)} async-done(((bf16[4,2,64,128]{3,2,1,0:T(8,128)(2,1)}), bf16[4,64,64,128]{3,2,1,0:T(8,128)(2,1)}) %all-gather.6.cloned.1.call-update) | async-done | bytes 4194320 | tf_op jit(solution)/shard_map/all_gather | solution.py:68
  94.4 4.4 %fusion.94 = (bf16[1,64,64,128]{3,2,1,0:T(8,128)(2,1)S(1)}, bf16[1,64,64,128]{3,2,1,0:T(8,128)(2,1)}, bf16[1,64,64,128]{3,2,1,0:T(8,128)(2,1)}, bf16[1,64,64,128]{3,2,1,0:T(8,128)(2,1)}) fusion(bf16[4,64,64,128]{3,2,1,0:T(8,128)(2,1)} %all-gather.6.cloned.1.call-done), kind=kLoop, calls=%fused_computation.176 | loop fusion | bytes 8388608 | tf_op jit(solution)/shard_map/slice | solution.py:82
  99.6 3.6 %fusion.106 = (f32[512]{0:T(512)S(1)}, f32[512,2048]{0,1:T(8,128)}) fusion(bf16[2048,128]{1,0:T(8,128)(2,1)S(1)} %bitcast.252, bf16[512,512]{1,0:T(8,128)(2,1)} %param.8, pred[512,2048]{0,1:T(32,128)(4,1)S(1)} %copy-done.19, s32[512]{0:T(512)S(1)} %copy-done.37, s32[2048]{0:T(1024)S(1)} %copy-done.32), kind=kOutput, calls=%fused_computation.188 | convolution fusion | flops 273677824 | bytes 5910528 | tf_op jit(solution)/shard_map/qd,kd->qk/dot_general | solution.py:89
  103.3 1.5 fusion.64
  104.8 1.7 fusion.78
  106.5 2.1 %fusion.96 = (bf16[32,1,1,64,128]{4,3,2,0,1:T(8,128)(2,1)}, bf16[32,1,1,64,128]{4,3,2,0,1:T(8,128)(2,1)S(1)}) fusion(bf16[32,1,2,64,128]{4,3,2,0,1:T(8,128)(2,1)} %bitcast.227), kind=kLoop, calls=%fused_computation.178 | loop fusion | bytes 2097152 | tf_op jit(solution)/shard_map/slice | solution.py:87
  108.6 3.6 %fusion.104 = (f32[512]{0:T(512)S(1)}, f32[512,2048]{0,1:T(8,128)}) fusion(bf16[2048,128]{1,0:T(8,128)(2,1)S(1)} %bitcast.253, bf16[512,512]{1,0:T(8,128)(2,1)} %param.8, pred[512,2048]{0,1:T(32,128)(4,1)S(1)} %copy-done.18, s32[512]{0:T(512)S(1)} %copy-done.37, s32[2048]{0:T(1024)S(1)} %copy-done.31), kind=kOutput, calls=%fused_computation.186 | convolution fusion | flops 273677824 | bytes 5910528 | tf_op jit(solution)/shard_map/qd,kd->qk/dot_general | solution.py:89
  112.5 2.2 %fusion.76 = f32[8,64,128,1]{2,1,3,0:T(8,128)} fusion(f32[8,64,4,64]{1,3,2,0:T(8,128)S(1)} %get-tuple-element.68, bf16[2,8,4,64,128]{4,3,2,1,0:T(8,128)(2,1)} %bitcast.234, f32[8,64]{1,0:T(8,128)S(1)} %max.47), kind=kOutput, calls=%fused_computation.70 | convolution fusion | flops 33816576 | bytes 1312768 | tf_op jit(solution)/shard_map/wojf,wjfl->wol/dot_general | solution.py:36
  114.7 2.1 %fusion.97 = (bf16[32,1,1,64,128]{4,3,2,0,1:T(8,128)(2,1)}, bf16[32,1,1,64,128]{4,3,2,0,1:T(8,128)(2,1)S(1)}) fusion(bf16[32,1,2,64,128]{4,3,2,0,1:T(8,128)(2,1)} %bitcast.226), kind=kLoop, calls=%fused_computation.179 | loop fusion | bytes 2097152 | tf_op jit(solution)/shard_map/slice | solution.py:87
  116.8 3.7 %fusion.102 = (f32[512]{0:T(512)S(1)}, f32[512,2048]{0,1:T(8,128)}) fusion(bf16[2048,128]{1,0:T(8,128)(2,1)S(1)} %bitcast.254, bf16[512,512]{1,0:T(8,128)(2,1)} %param.8, pred[512,2048]{0,1:T(32,128)(4,1)S(1)} %copy-done.17, s32[512]{0:T(512)S(1)} %copy-done.37, s32[2048]{0:T(1024)S(1)} %copy-done.30), kind=kOutput, calls=%fused_computation.184 | convolution fusion | flops 273677824 | bytes 5910528 | tf_op jit(solution)/shard_map/qd,kd->qk/dot_general | solution.py:89
  120.8 2.2 %fusion.74 = f32[8,64,128,1]{2,1,3,0:T(8,128)} fusion(f32[8,64,4,64]{1,3,2,0:T(8,128)S(1)} %get-tuple-element.64, bf16[2,8,4,64,128]{4,3,2,1,0:T(8,128)(2,1)} %bitcast.232, f32[8,64]{1,0:T(8,128)S(1)} %max.49), kind=kOutput, calls=%fused_computation.69 | convolution fusion | flops 33816576 | bytes 1312768 | tf_op jit(solution)/shard_map/wojf,wjfl->wol/dot_general | solution.py:36
  123.9 3.7 %fusion.100 = (f32[512]{0:T(512)S(1)}, f32[512,2048]{0,1:T(8,128)}) fusion(bf16[2048,128]{1,0:T(8,128)(2,1)S(1)} %bitcast.251, bf16[512,512]{1,0:T(8,128)(2,1)} %param.8, pred[512,2048]{0,1:T(32,128)(4,1)S(1)} %copy-done.16, s32[512]{0:T(512)S(1)} %copy-done.37, s32[2048]{0:T(1024)S(1)} %copy-done.29), kind=kOutput, calls=%fused_computation.182 | convolution fusion | flops 273677824 | bytes 5910528 | tf_op jit(solution)/shard_map/qd,kd->qk/dot_general | solution.py:89
  129.1 3.0 %fusion = f32[512]{0:T(512)S(1)} fusion(f32[512,2048]{0,1:T(8,128)} %get-tuple-element.70, f32[512]{0:T(512)S(1)} %max.44), kind=kLoop, calls=%fused_computation.15 | loop fusion | flops 2096640 | bytes 4198400 | tf_op jit(solution)/shard_map/reduce_sum | solution.py:28
  140.5 35.2 %all-gather.4.cloned.1.call-done = bf16[512,4096]{0,1:T(8,128)(2,1)} async-done(((bf16[512,512]{0,1:T(8,128)(2,1)}), bf16[512,4096]{0,1:T(8,128)(2,1)}) %all-gather.4.cloned.1.call-update) | async-done | bytes 4194320 | tf_op jit(solution)/shard_map/all_gather | solution.py:131
  175.7 6.6 %convolution_convert_fusion = bf16[512,512]{1,0:T(8,128)(2,1)} fusion(bf16[512,4096]{0,1:T(8,128)(2,1)} %all-gather.4.cloned.1.call-done, bf16[4096,512]{1,0:T(8,128)(2,1)} %param.15), kind=kOutput, calls=%fused_computation.43 | convolution fusion | flops 2147745792 | bytes 8912896 | tf_op jit(solution)/shard_map/dot_general | solution.py:130
  (210 shorter events, 37.8 us)
Async XLA Ops:
  6.5 13.9 %copy-start.28 = (s32[4,32,1]{1,2,0:T(1,128)S(1)}, s32[4,32,1]{1,2,0:T(1,128)}, u32[]{:S(2)}) copy-start(s32[4,32,1]{1,2,0:T(1,128)} %param.13) | copy-start | bytes 1540
  6.5 13.4 %copy-start.35 = (s32[4,4]{1,0:T(4,128)S(1)}, s32[4,4]{1,0:T(4,128)}, u32[]{:S(2)}) copy-start(s32[4,4]{1,0:T(4,128)} %param.11) | copy-start | bytes 196
  6.5 14.2 %copy-start.36 = (s32[4,32]{1,0:T(4,128)S(1)}, s32[4,32]{1,0:T(4,128)}, u32[]{:S(2)}) copy-start(s32[4,32]{1,0:T(4,128)} %param.14) | copy-start | bytes 1540
  6.5 87.8 %all-gather.6.cloned.1.call-start = ((), (), s32[]{:S(2)}) async-start(), calls=%async_computation.1 | async-start | bytes 4325376 | tf_op jit(solution)/shard_map/all_gather | solution.py:68
  11.3 164.4 %all-gather.4.cloned.1.call-start = ((), (), s32[]{:S(2)}) async-start(), calls=%async_computation | async-start | bytes 4718592 | tf_op jit(solution)/shard_map/all_gather | solution.py:131
  12.4 35.8 %collective-permute-start = (bf16[2,512,128]{2,1,0:T(8,128)(2,1)S(1)}, bf16[2,512,128]{2,1,0:T(8,128)(2,1)S(1)}, u32[]{:S(2)}, u32[]{:S(2)}) collective-permute-start(bf16[2,512,128]{2,1,0:T(8,128)(2,1)S(1)} %pad_maximum_fusion.2), channel_id=1, source_target_pairs={{0,8},{8,16},{16,24},{24,32},{32,40},{40,48},{48,56},{56,64},{64,7... | collective-permute-start | bytes 786440 | tf_op jit(solution)/shard_map/ppermute | solution.py:15
  35.9 11.5 %copy-start.22 = (bf16[512,512]{1,0:T(8,128)(2,1)S(1)}, bf16[512,512]{1,0:T(8,128)(2,1)}, u32[]{:S(2)}) copy-start(bf16[512,512]{1,0:T(8,128)(2,1)} %param.8) | copy-start | bytes 1572868
  35.9 12.2 %copy-start.14 = (bf16[512,128]{1,0:T(8,128)(2,1)S(1)}, bf16[512,128]{1,0:T(8,128)(2,1)}, u32[]{:S(2)}) copy-start(bf16[512,128]{1,0:T(8,128)(2,1)} %param.10) | copy-start | bytes 393220
  35.9 12.2 %copy-start.15 = (bf16[512,128]{1,0:T(8,128)(2,1)S(1)}, bf16[512,128]{1,0:T(8,128)(2,1)}, u32[]{:S(2)}) copy-start(bf16[512,128]{1,0:T(8,128)(2,1)} %param.9) | copy-start | bytes 393220
  55.1 6.1 %copy-start.24 = (pred[64,4,64]{0,2,1:T(8,128)(4,1)S(1)}, pred[64,4,64]{0,2,1:T(8,128)(4,1)}, u32[]{:S(2)}) copy-start(pred[64,4,64]{0,2,1:T(8,128)(4,1)} %get-tuple-element.24) | copy-start | bytes 49156
  55.1 6.1 %copy-start.38 = (pred[8,4]{1,0:T(8,128)(4,1)S(1)}, pred[8,4]{1,0:T(8,128)(4,1)}, u32[]{:S(2)}) copy-start(pred[8,4]{1,0:T(8,128)(4,1)} %get-tuple-element.52) | copy-start | bytes 100
  61.6 38.0 %copy-start.32 = (s32[2048]{0:T(1024)S(1)}, s32[2048]{0:T(1024)}, u32[]{:S(2)}) copy-start(s32[2048]{0:T(1024)} %add.293) | copy-start | bytes 24580
  61.6 38.0 %copy-start.37 = (s32[512]{0:T(512)S(1)}, s32[512]{0:T(512)}, u32[]{:S(2)}) copy-start(s32[512]{0:T(512)} %iota_add_fusion.4) | copy-start | bytes 6148
  94.4 5.3 %copy-start.19 = (pred[512,2048]{0,1:T(32,128)(4,1)S(1)}, pred[512,2048]{0,1:T(32,128)(4,1)}, u32[]{:S(2)}) copy-start(pred[512,2048]{0,1:T(32,128)(4,1)} %reshape.1051) | copy-start | bytes 3145732
  99.6 8.9 %copy-start.31 = (s32[2048]{0:T(1024)S(1)}, s32[2048]{0:T(1024)}, u32[]{:S(2)}) copy-start(s32[2048]{0:T(1024)} %add.307) | copy-start | bytes 24580
  103.3 5.3 %copy-start.18 = (pred[512,2048]{0,1:T(32,128)(4,1)S(1)}, pred[512,2048]{0,1:T(32,128)(4,1)}, u32[]{:S(2)}) copy-start(pred[512,2048]{0,1:T(32,128)(4,1)} %reshape.1054) | copy-start | bytes 3145732
  108.6 8.2 %copy-start.30 = (s32[2048]{0:T(1024)S(1)}, s32[2048]{0:T(1024)}, u32[]{:S(2)}) copy-start(s32[2048]{0:T(1024)} %add.314) | copy-start | bytes 24580
  116.8 6.2 %copy-start.4 = (bf16[1,64,64,128]{3,2,1,0:T(8,128)(2,1)S(1)}, bf16[1,64,64,128]{3,2,1,0:T(8,128)(2,1)}, u32[]{:S(2)}) copy-start(bf16[1,64,64,128]{3,2,1,0:T(8,128)(2,1)} %get-tuple-element.8) | copy-start | bytes 3145732
  116.8 7.0 %copy-start.29 = (s32[2048]{0:T(1024)S(1)}, s32[2048]{0:T(1024)}, u32[]{:S(2)}) copy-start(s32[2048]{0:T(1024)} %add.321) | copy-start | bytes 24580
  123.8 4.7 %copy-start.20 = (f32[8,64,128,1]{2,1,3,0:T(8,128)S(1)}, f32[8,64,128,1]{2,1,3,0:T(8,128)}, u32[]{:S(2)}) copy-start(f32[8,64,128,1]{2,1,3,0:T(8,128)} %fusion.76) | copy-start | bytes 786436
  123.8 4.8 %copy-start.34 = (f32[512]{0:T(512)S(1)}, f32[512]{0:T(512)}, u32[]{:S(2)}) copy-start(f32[512]{0:T(512)} %reduce_max.98) | copy-start | bytes 6148
  123.9 4.9 %copy-start.21 = (f32[8,64,128,1]{2,1,3,0:T(8,128)S(1)}, f32[8,64,128,1]{2,1,3,0:T(8,128)}, u32[]{:S(2)}) copy-start(f32[8,64,128,1]{2,1,3,0:T(8,128)} %fusion.74) | copy-start | bytes 786436
  128.9 6.9 %copy-start.10 = (bf16[32,1,1,64,128]{4,3,2,0,1:T(8,128)(2,1)S(1)}, bf16[32,1,1,64,128]{4,3,2,0,1:T(8,128)(2,1)}, u32[]{:S(2)}) copy-start(bf16[32,1,1,64,128]{4,3,2,0,1:T(8,128)(2,1)} %get-tuple-element.9) | copy-start | bytes 1572868
  129.1 4.7 %copy-start.2 = (f32[512,2048]{0,1:T(8,128)S(1)}, f32[512,2048]{0,1:T(8,128)}, u32[]{:S(2)}) copy-start(f32[512,2048]{0,1:T(8,128)} %get-tuple-element.62) | copy-start | bytes 12582916
  (21 other events, 61.5 us)
Sparse Core Ops, SparseCore 0:
  11.4 82.9 all-gather.5
  140.6 35.0 all-gather.3
where the time goes:
time: 190 us; the launch traced here: 189 us
  waiting for transfers between devices  68 us (36%)
  local copies, waits for them, and re-layouts  56.4 us (30%)
  matrix products  33.1 us (17%)
  between operations  14.1 us (7%)
  other arithmetic  13.2 us (7%)
  starting transfers between devices  4.43 us (2%)
    all_gather x1, waiting for transfers between devices, shards(): lax.all_gather(attended, 'head', axis=1, tiled=True)  35.2 us
    all_gather x1, waiting for transfers between devices, shards(): gathered = lax.all_gather(block_rows[:, None], 'ctx', axis=1, tiled=True)  32.7 us
    reshape x4, local copies, waits for them, and re-layouts, shards(): vert_mask = jnp.broadcast_to(block_mask[:, None, :, None], (per_dev, BLOC...  18.9 us
    dot_general x4, matrix products, shards(): jnp.einsum('qd,kd->qk', query_head, vert_keys, preferred_element_type=jnp...  14.6 us
    unnamed x88, local copies, waits for them, and re-layouts  6.68 us
    dot_general x1, matrix products, shards(): jnp.dot(lax.all_gather(attended, 'head', axis=1, tiled=True), out_weight,...  6.61 us
    dot_general x4, matrix products, attend(): jnp.einsum('wojf,wjfl->wol', slash_probability, diagonal_values, preferre...  6.35 us
    slice x4, local copies, waits for them, and re-layouts, shards(): vertical[:, :, 1].reshape(slot_count * BLOCK_TOKENS, HEAD_SIZE)  5.9 us
  transfers between devices with their start and end apart: 3, of which 2 were waited for; matrix products, arithmetic and copies ran while one was open for 22% of the time, Pallas kernels for 0%

commit v1 on v0

--- a/solution.py
+++ b/solution.py
@@ -65,7 +65,11 @@
     mine_picks = lax.dynamic_index_in_dim(head_picks, device_rank, 1, keepdims=False)
     chosen_local = jnp.take_along_axis(mine_union[head_group], mine_picks, axis=1)
     block_rows = local_blocks[:, chosen_local, :, head_group[:, None], :]
-    gathered = lax.all_gather(block_rows[:, None], "ctx", axis=1, tiled=True)
+    part = block_rows[:, None]
+    peers = lax.axis_size("ctx")
+    blocks = jnp.stack([part for _ in range(peers)])
+    blocks = lax.all_to_all(blocks, "ctx", split_axis=0, concat_axis=0)
+    gathered = jnp.concatenate(blocks, axis=1)
     slot_block = owner_base[None] + jnp.take_along_axis(
         union_blocks[head_group], head_picks, axis=2
     )

time: 190 us -> 234 us (1.23)
  waiting for transfers between devices: 68 us -> 101 us
  starting transfers between devices: 4.43 us -> 15.3 us
    ppermute x1, waiting for transfers between devices: 0.01 us -> 62.5 us  [from_behind(): return lax.ppermute(array, axis, pairs)]
    all_gather x1 -> x0, waiting for transfers between devices: 32.7 us -> none  [shards(): gathered = lax.all_gather(block_rows[:, None], 'ctx', axis=1, tiled=True)]
    all_to_all x0 -> x1, starting transfers between devices: none -> 12.1 us  [shards(): blocks = lax.all_to_all(blocks, 'ctx', split_axis=0, concat_axis=0)]
    squeeze x0 -> x1, local copies, waits for them, and re-layouts: none -> 5.04 us  [shards(): vertical = gathered[source_of[head_index]]]
    slice x1 -> x0, local copies, waits for them, and re-layouts: 4.36 us -> none  [shards(): vertical = gathered[source_of[head_index]]]
    all_gather x1, waiting for transfers between devices: 35.2 us -> 38.6 us  [shards(): lax.all_gather(attended, 'head', axis=1, tiled=True)]
    another operation x0 -> x1, local copies, waits for them, and re-layouts: none -> 3.03 us  [shards(): blocks = jnp.stack([part for _ in range(peers)])]
    unnamed x88 -> x90, local copies, waits for them, and re-layouts: 6.68 us -> 6.67 us
  transfers between devices with their start and end apart: 3 -> 3, of which waited for: 2 -> 2; matrix products, arithmetic and copies ran while one was open for 22% -> 17% of each run, Pallas kernels for 0% -> 0%
where the time goes in v1:
time: 234 us
  waiting for transfers between devices  101 us (43%)
  local copies, waits for them, and re-layouts  58.7 us (25%)
  matrix products  33 us (14%)
  starting transfers between devices  15.3 us (7%)
  between operations  14.2 us (6%)
  other arithmetic  11.5 us (5%)
    ppermute x1, waiting for transfers between devices, from_behind(): return lax.ppermute(array, axis, pairs)  62.5 us
    all_gather x1, waiting for transfers between devices, shards(): lax.all_gather(attended, 'head', axis=1, tiled=True)  38.6 us
    reshape x4, local copies, waits for them, and re-layouts, shards(): vert_mask = jnp.broadcast_to(block_mask[:, None, :, None], (per_dev, BLOC...  18.9 us
    dot_general x4, matrix products, shards(): jnp.einsum('qd,kd->qk', query_head, vert_keys, preferred_element_type=jnp...  14.6 us
    all_to_all x1, starting transfers between devices, shards(): blocks = lax.all_to_all(blocks, 'ctx', split_axis=0, concat_axis=0)  12.1 us
    unnamed x90, local copies, waits for them, and re-layouts  6.67 us
    dot_general x1, matrix products, shards(): jnp.dot(lax.all_gather(attended, 'head', axis=1, tiled=True), out_weight,...  6.61 us
    dot_general x4, matrix products, attend(): jnp.einsum('wojf,wjfl->wol', slash_probability, diagonal_values, preferre...  6.35 us
  transfers between devices with their start and end apart: 3, of which 2 were waited for; matrix products, arithmetic and copies ran while one was open for 17% of the time, Pallas kernels for 0%

profile of v1, /device:TPU:1, one launch (start us, length us, event | category | flops | bytes accessed | tf_op | source)
XLA Modules:
  0.0 233.8 jit_solution(8045088279705437814)
XLA Ops:
  10.6 3.0 %stack.21 = bf16[32,4,1,1,2,64,128]{6,5,4,3,2,1,0:T(8,128)(2,1)} broadcast(bf16[4,2,64,128]{3,2,1,0:T(8,128)(2,1)S(1)} %gather_fusion), dimensions={1,4,5,6} | broadcast | bytes 4325376 | tf_op jit(solution)/shard_map/stack | solution.py:70
  13.6 12.1 %all-to-all-start = ((bf16[32,4,1,1,2,64,128]{6,5,4,3,2,1,0:T(8,128)(2,1)}), bf16[32,4,1,1,2,64,128]{6,5,4,3,2,1,0:T(8,128)(2,1)}, u32[]{:S(2)}, u32[]{:S(2)}) async-start(bf16[32,4,1,1,2,64,128]{6,5,4,3,2,1,0:T(8,128)(2,1)} %stack.21), calls=%async_computation | async-start | bytes 8388608 | tf_op jit(solution)/shard_map/all_to_all | solution.py:71
  25.9 3.1 %collective-permute-start = (bf16[2,512,128]{2,1,0:T(8,128)(2,1)S(1)}, bf16[2,512,128]{2,1,0:T(8,128)(2,1)S(1)}, u32[]{:S(2)}, u32[]{:S(2)}) collective-permute-start(bf16[2,512,128]{2,1,0:T(8,128)(2,1)S(1)} %pad_maximum_fusion.2), channel_id=1, source_target_pairs={{0,8},{8,16},{16,24},{24,32},{32,40},{40,48},{48,56},{56,64},{64,7... | collective-permute-start | bytes 786440 | tf_op jit(solution)/shard_map/ppermute | solution.py:15
  29.2 1.5 gather_fusion.5
  34.5 4.7 %reshape.1066 = pred[512,2048]{0,1:T(32,128)(4,1)} reshape(pred[8,64,32,64]{1,0,3,2:T(8,128)(4,1)S(1)} %broadcast_in_dim.26) | data formatting | bytes 2097152 | tf_op jit(solution)/shard_map/reshape | solution.py:102
  40.6 4.7 %reshape.1070 = pred[512,2048]{0,1:T(32,128)(4,1)} reshape(pred[8,64,32,64]{1,0,3,2:T(8,128)(4,1)S(1)} %broadcast_in_dim.30) | data formatting | bytes 2097152 | tf_op jit(solution)/shard_map/reshape | solution.py:102
  46.8 4.7 %reshape.1073 = pred[512,2048]{0,1:T(32,128)(4,1)} reshape(pred[8,64,32,64]{1,0,3,2:T(8,128)(4,1)S(1)} %broadcast_in_dim.31) | data formatting | bytes 2097152 | tf_op jit(solution)/shard_map/reshape | solution.py:102
  52.8 4.7 %reshape.1076 = pred[512,2048]{0,1:T(32,128)(4,1)} reshape(pred[8,64,32,64]{1,0,3,2:T(8,128)(4,1)S(1)} %broadcast_in_dim.32) | data formatting | bytes 2097152 | tf_op jit(solution)/shard_map/reshape | solution.py:102
  59.0 62.5 %collective-permute-done = bf16[2,512,128]{2,1,0:T(8,128)(2,1)S(1)} collective-permute-done((bf16[2,512,128]{2,1,0:T(8,128)(2,1)S(1)}, bf16[2,512,128]{2,1,0:T(8,128)(2,1)S(1)}, u32[]{:S(2)}, u32[]{:S(2)}) %collective-permute-start) | collective-permute-done | bytes 262176 | tf_op jit(solution)/shard_map/ppermute | solution.py:15
  130.6 1.7 gather_fusion.4
  135.0 5.0 %slice_bitcast_fusion.3 = (bf16[32,1,2,64,128]{4,3,2,0,1:T(8,128)(2,1)S(1)}, bf16[32,1,2,64,128]{4,3,2,0,1:T(8,128)(2,1)}, bf16[32,1,2,64,128]{4,3,2,0,1:T(8,128)(2,1)}, bf16[32,1,2,64,128]{4,3,2,0,1:T(8,128)(2,1)}) fusion(bf16[4,32,1,1,2,64,128]{6,5,4,3,2,0,1:T(8,128)(2,1)} %bitcast.16), kind=kLoop, calls=%fused_computation.59 | loop fusion | bytes 8388608 | tf_op jit(solution)/shard_map/squeeze | solution.py:86
  140.9 3.6 %fusion.105 = (f32[512]{0:T(512)S(1)}, f32[512,2048]{0,1:T(8,128)}) fusion(bf16[2048,128]{1,0:T(8,128)(2,1)S(1)} %bitcast.253, bf16[512,512]{1,0:T(8,128)(2,1)} %param.8, pred[512,2048]{0,1:T(32,128)(4,1)S(1)} %copy-done.19, s32[512]{0:T(512)S(1)} %copy-done.38, s32[2048]{0:T(1024)S(1)} %copy-done.32), kind=kOutput, calls=%fused_computation.191 | convolution fusion | flops 273677824 | bytes 5910528 | tf_op jit(solution)/shard_map/qd,kd->qk/dot_general | solution.py:93
  144.6 1.5 fusion.64
  146.1 1.7 fusion.78
  147.8 2.1 fusion.95
  149.9 3.6 %fusion.103 = (f32[512]{0:T(512)S(1)}, f32[512,2048]{0,1:T(8,128)}) fusion(bf16[2048,128]{1,0:T(8,128)(2,1)S(1)} %bitcast.254, bf16[512,512]{1,0:T(8,128)(2,1)} %param.8, pred[512,2048]{0,1:T(32,128)(4,1)S(1)} %copy-done.18, s32[512]{0:T(512)S(1)} %copy-done.38, s32[2048]{0:T(1024)S(1)} %copy-done.31), kind=kOutput, calls=%fused_computation.189 | convolution fusion | flops 273677824 | bytes 5910528 | tf_op jit(solution)/shard_map/qd,kd->qk/dot_general | solution.py:93
  153.8 2.2 fusion.76
  156.0 2.1 fusion.96
  158.1 3.7 %fusion.101 = (f32[512]{0:T(512)S(1)}, f32[512,2048]{0,1:T(8,128)}) fusion(bf16[2048,128]{1,0:T(8,128)(2,1)S(1)} %bitcast.255, bf16[512,512]{1,0:T(8,128)(2,1)} %param.8, pred[512,2048]{0,1:T(32,128)(4,1)S(1)} %copy-done.17, s32[512]{0:T(512)S(1)} %copy-done.38, s32[2048]{0:T(1024)S(1)} %copy-done.30), kind=kOutput, calls=%fused_computation.187 | convolution fusion | flops 273677824 | bytes 5910528 | tf_op jit(solution)/shard_map/qd,kd->qk/dot_general | solution.py:93
  162.1 2.2 fusion.74
  165.2 3.7 %fusion.99 = (f32[512]{0:T(512)S(1)}, f32[512,2048]{0,1:T(8,128)}) fusion(bf16[2048,128]{1,0:T(8,128)(2,1)S(1)} %bitcast.252, bf16[512,512]{1,0:T(8,128)(2,1)} %param.8, pred[512,2048]{0,1:T(32,128)(4,1)S(1)} %copy-done.16, s32[512]{0:T(512)S(1)} %copy-done.38, s32[2048]{0:T(1024)S(1)} %copy-done.29), kind=kOutput, calls=%fused_computation.185 | convolution fusion | flops 273677824 | bytes 5910528 | tf_op jit(solution)/shard_map/qd,kd->qk/dot_general | solution.py:93
  170.4 3.0 %fusion = f32[512]{0:T(512)S(1)} fusion(f32[512,2048]{0,1:T(8,128)} %get-tuple-element.70, f32[512]{0:T(512)S(1)} %max.44), kind=kLoop, calls=%fused_computation.15 | loop fusion | flops 2096640 | bytes 4198400 | tf_op jit(solution)/shard_map/reduce_sum | solution.py:28
  181.8 38.6 %all-gather.2.cloned.1.call-done = bf16[512,4096]{0,1:T(8,128)(2,1)} async-done(((bf16[512,512]{0,1:T(8,128)(2,1)}), bf16[512,4096]{0,1:T(8,128)(2,1)}) %all-gather.2.cloned.1.call-update) | async-done | bytes 4194320 | tf_op jit(solution)/shard_map/all_gather | solution.py:135
  220.3 6.6 %convolution_convert_fusion = bf16[512,512]{1,0:T(8,128)(2,1)} fusion(bf16[512,4096]{0,1:T(8,128)(2,1)} %all-gather.2.cloned.1.call-done, bf16[4096,512]{1,0:T(8,128)(2,1)} %param.15), kind=kOutput, calls=%fused_computation.43 | convolution fusion | flops 2147745792 | bytes 8912896 | tf_op jit(solution)/shard_map/dot_general | solution.py:134
  (212 shorter events, 37.3 us)
Async XLA Ops:
  13.6 12.2 %copy-start.14 = (bf16[512,128]{1,0:T(8,128)(2,1)S(1)}, bf16[512,128]{1,0:T(8,128)(2,1)}, u32[]{:S(2)}) copy-start(bf16[512,128]{1,0:T(8,128)(2,1)} %param.10) | copy-start | bytes 393220
  13.6 12.2 %copy-start.15 = (bf16[512,128]{1,0:T(8,128)(2,1)S(1)}, bf16[512,128]{1,0:T(8,128)(2,1)}, u32[]{:S(2)}) copy-start(bf16[512,128]{1,0:T(8,128)(2,1)} %param.9) | copy-start | bytes 393220
  13.6 15.4 %copy-start.28 = (s32[4,32,1]{1,2,0:T(1,128)S(1)}, s32[4,32,1]{1,2,0:T(1,128)}, u32[]{:S(2)}) copy-start(s32[4,32,1]{1,2,0:T(1,128)} %param.13) | copy-start | bytes 1540
  13.6 15.5 %copy-start.36 = (s32[1,32,2]{1,2,0:T(2,128)S(1)}, s32[1,32,2]{1,2,0:T(2,128)}, u32[]{:S(2)}) copy-start(s32[1,32,2]{1,2,0:T(2,128)} %param.12) | copy-start | bytes 772
  13.6 17.2 %copy-start.35 = (s32[4,4]{1,0:T(4,128)S(1)}, s32[4,4]{1,0:T(4,128)}, u32[]{:S(2)}) copy-start(s32[4,4]{1,0:T(4,128)} %param.11) | copy-start | bytes 196
  13.6 18.0 %copy-start.37 = (s32[4,32]{1,0:T(4,128)S(1)}, s32[4,32]{1,0:T(4,128)}, u32[]{:S(2)}) copy-start(s32[4,32]{1,0:T(4,128)} %param.14) | copy-start | bytes 1540
  13.6 121.4 %all-to-all-start = ((bf16[32,4,1,1,2,64,128]{6,5,4,3,2,1,0:T(8,128)(2,1)}), bf16[32,4,1,1,2,64,128]{6,5,4,3,2,1,0:T(8,128)(2,1)}, u32[]{:S(2)}, u32[]{:S(2)}) async-start(bf16[32,4,1,1,2,64,128]{6,5,4,3,2,1,0:T(8,128)(2,1)} %stack.21), calls=%async_computation | async-start | bytes 8388608 | tf_op jit(solution)/shard_map/all_to_all | solution.py:71
  25.8 194.6 %all-gather.2.cloned.1.call-start = ((), (), s32[]{:S(2)}) async-start(), calls=%async_computation.1 | async-start | bytes 4718592 | tf_op jit(solution)/shard_map/all_gather | solution.py:135
  25.9 95.6 %collective-permute-start = (bf16[2,512,128]{2,1,0:T(8,128)(2,1)S(1)}, bf16[2,512,128]{2,1,0:T(8,128)(2,1)S(1)}, u32[]{:S(2)}, u32[]{:S(2)}) collective-permute-start(bf16[2,512,128]{2,1,0:T(8,128)(2,1)S(1)} %pad_maximum_fusion.2), channel_id=1, source_target_pairs={{0,8},{8,16},{16,24},{24,32},{32,40},{40,48},{48,56},{56,64},{64,7... | collective-permute-start | bytes 786440 | tf_op jit(solution)/shard_map/ppermute | solution.py:15
  46.7 11.5 %copy-start.22 = (bf16[512,512]{1,0:T(8,128)(2,1)S(1)}, bf16[512,512]{1,0:T(8,128)(2,1)}, u32[]{:S(2)}) copy-start(bf16[512,512]{1,0:T(8,128)(2,1)} %param.8) | copy-start | bytes 1572868
  57.5 65.8 %copy-start.27 = (pred[64,4,64]{0,2,1:T(8,128)(4,1)S(1)}, pred[64,4,64]{0,2,1:T(8,128)(4,1)}, u32[]{:S(2)}) copy-start(pred[64,4,64]{0,2,1:T(8,128)(4,1)} %get-tuple-element.21) | copy-start | bytes 49156
  57.5 65.8 %copy-start.42 = (pred[8,4]{1,0:T(8,128)(4,1)S(1)}, pred[8,4]{1,0:T(8,128)(4,1)}, u32[]{:S(2)}) copy-start(pred[8,4]{1,0:T(8,128)(4,1)} %get-tuple-element.49) | copy-start | bytes 100
  128.4 6.1 %copy-start.24 = (pred[64,4,64]{0,2,1:T(8,128)(4,1)S(1)}, pred[64,4,64]{0,2,1:T(8,128)(4,1)}, u32[]{:S(2)}) copy-start(pred[64,4,64]{0,2,1:T(8,128)(4,1)} %get-tuple-element.24) | copy-start | bytes 49156
  128.5 6.1 %copy-start.39 = (pred[8,4]{1,0:T(8,128)(4,1)S(1)}, pred[8,4]{1,0:T(8,128)(4,1)}, u32[]{:S(2)}) copy-start(pred[8,4]{1,0:T(8,128)(4,1)} %get-tuple-element.52) | copy-start | bytes 100
  135.0 5.9 %copy-start.19 = (pred[512,2048]{0,1:T(32,128)(4,1)S(1)}, pred[512,2048]{0,1:T(32,128)(4,1)}, u32[]{:S(2)}) copy-start(pred[512,2048]{0,1:T(32,128)(4,1)} %reshape.1066) | copy-start | bytes 3145732
  135.0 5.9 %copy-start.32 = (s32[2048]{0:T(1024)S(1)}, s32[2048]{0:T(1024)}, u32[]{:S(2)}) copy-start(s32[2048]{0:T(1024)} %add.293) | copy-start | bytes 24580
  135.0 5.9 %copy-start.38 = (s32[512]{0:T(512)S(1)}, s32[512]{0:T(512)}, u32[]{:S(2)}) copy-start(s32[512]{0:T(512)} %iota_add_fusion.4) | copy-start | bytes 6148
  140.9 8.9 %copy-start.31 = (s32[2048]{0:T(1024)S(1)}, s32[2048]{0:T(1024)}, u32[]{:S(2)}) copy-start(s32[2048]{0:T(1024)} %add.307) | copy-start | bytes 24580
  144.6 5.3 %copy-start.18 = (pred[512,2048]{0,1:T(32,128)(4,1)S(1)}, pred[512,2048]{0,1:T(32,128)(4,1)}, u32[]{:S(2)}) copy-start(pred[512,2048]{0,1:T(32,128)(4,1)} %reshape.1070) | copy-start | bytes 3145732
  149.9 8.2 %copy-start.30 = (s32[2048]{0:T(1024)S(1)}, s32[2048]{0:T(1024)}, u32[]{:S(2)}) copy-start(s32[2048]{0:T(1024)} %add.314) | copy-start | bytes 24580
  158.1 6.2 %copy-start.4 = (bf16[32,1,2,64,128]{4,3,2,0,1:T(8,128)(2,1)S(1)}, bf16[32,1,2,64,128]{4,3,2,0,1:T(8,128)(2,1)}, u32[]{:S(2)}) copy-start(bf16[32,1,2,64,128]{4,3,2,0,1:T(8,128)(2,1)} %get-tuple-element.6) | copy-start | bytes 3145732
  158.1 7.0 %copy-start.29 = (s32[2048]{0:T(1024)S(1)}, s32[2048]{0:T(1024)}, u32[]{:S(2)}) copy-start(s32[2048]{0:T(1024)} %add.321) | copy-start | bytes 24580
  165.2 4.9 %copy-start.21 = (f32[8,64,128,1]{2,1,3,0:T(8,128)S(1)}, f32[8,64,128,1]{2,1,3,0:T(8,128)}, u32[]{:S(2)}) copy-start(f32[8,64,128,1]{2,1,3,0:T(8,128)} %fusion.74) | copy-start | bytes 786436
  170.2 6.9 %copy-start.10 = (bf16[32,1,1,64,128]{4,3,2,0,1:T(8,128)(2,1)S(1)}, bf16[32,1,1,64,128]{4,3,2,0,1:T(8,128)(2,1)}, u32[]{:S(2)}) copy-start(bf16[32,1,1,64,128]{4,3,2,0,1:T(8,128)(2,1)} %get-tuple-element.9) | copy-start | bytes 1572868
  (22 other events, 69.0 us)
Sparse Core Ops, SparseCore 0:
  181.9 38.4 all-gather.1
